TPU v7x, 128 devices: a whole 4x4x4 slice. The times are simulated.
128 devices in a mesh: lat: 16 (over x, y_hi, core), lon: 8 (over y_lo, z).
Axes of the slice: x: 4, y: 4 (y_hi: 2, y_lo: 2; y = y_hi * 2 + y_lo), z: 4, core: 2. Of those that a mesh axis runs over, the one named last changes fastest.
Arguments:
- tokens: bfloat16 [256, 2048, 256], P('lat', 'lon'), may hold values from -16 to 16
- w_qkv: bfloat16 [256, 768], replicated, may hold values from -0.375 to 0.375
- w_out: bfloat16 [256, 256], replicated, may hold values from -0.375 to 0.375
Outputs:
- attended: bfloat16 [256, 2048, 256], P('lat', 'lon')
All inputs are finite; a program needn't handle non-finite values.
Results may differ from a plain program's by a relative error of at most 0.011.
Values may be sent and summed in bfloat16 or wider, within the bound.
No kernel may reach another device: no remote copies, remote signals or barrier semaphores. Data moves between devices by JAX's collectives and lax.ppermute only.
A program may use at most 320 MiB of HBM per device.

v0:
```python
import math

import jax
import jax.numpy as jnp
from jax import lax
from jax.sharding import PartitionSpec as P

HEADS = 8
GRID = 8


def attend(grid_block, w_qkv, w_out, layout, members):
    lead_shape = grid_block.shape[:-1]
    model_width = grid_block.shape[-1]
    head_size = model_width // HEADS
    qkv = jnp.dot(
        grid_block.reshape(-1, model_width), w_qkv, preferred_element_type=jnp.float32
    ).astype(jnp.bfloat16)
    qkv = qkv.reshape(lead_shape + (3, HEADS, head_size))
    query_part = qkv[..., 0, :, :]
    key_part = qkv[..., 1, :, :]
    value_part = qkv[..., 2, :, :]
    keyset = "xyz"[: len(members)]
    mapping = dict(zip(members, keyset))
    partner = "".join((mapping.get(letter, letter) for letter in layout))
    groups = "".join((letter for letter in layout if letter not in members))
    score_scale = 1.0 / math.sqrt(head_size)
    scores = (
        jnp.einsum(
            layout + "he," + partner + "he->" + groups + "h" + members + keyset,
            query_part,
            key_part,
            preferred_element_type=jnp.float32,
        )
        * score_scale
    )
    sum_axes = tuple(range(-len(members), 0))
    row_max = jnp.max(scores, axis=sum_axes, keepdims=True)
    exponent = jnp.exp(scores - row_max)
    weights = (exponent / jnp.sum(exponent, axis=sum_axes, keepdims=True)).astype(jnp.bfloat16)
    mixed = jnp.einsum(
        groups + "h" + members + keyset + "," + partner + "he->" + layout + "he",
        weights,
        value_part,
        preferred_element_type=jnp.float32,
    ).astype(jnp.bfloat16)
    flat_rows = mixed.reshape(-1, model_width)
    flat_rows = jnp.dot(flat_rows, w_out, preferred_element_type=jnp.float32).astype(jnp.bfloat16)
    return flat_rows.reshape(lead_shape + (model_width,))


def body(tokens, w_qkv, w_out):
    lat_count = lax.axis_size("lat")
    lon_count = lax.axis_size("lon")
    row_count, column_count, model_width = tokens.shape
    piece_rows = row_count // lat_count
    per_device = GRID // lon_count
    piece_cols = column_count // GRID
    lat_share = lat_count // GRID
    shaped = tokens.reshape(lat_count, piece_rows, per_device, lon_count, piece_cols, model_width)
    ordered = shaped.transpose(0, 3, 1, 2, 4, 5).reshape(
        lat_count * lon_count, piece_rows, per_device, piece_cols, model_width
    )
    arrived = lax.all_to_all(ordered, ("lat", "lon"), split_axis=0, concat_axis=0, tiled=True)
    item_count = arrived.shape[1]
    grid_block = arrived.reshape(
        GRID, lat_share, lon_count, item_count, per_device, piece_cols, model_width
    )
    finished = attend(grid_block, w_qkv, w_out, "gsjnlc", "gjl")
    processed = finished.reshape(
        lat_count * lon_count, item_count, per_device, piece_cols, model_width
    )
    returned = lax.all_to_all(processed, ("lat", "lon"), split_axis=0, concat_axis=0, tiled=True)
    result = returned.reshape(
        lat_count, lon_count, piece_rows, per_device, piece_cols, model_width
    ).transpose(0, 2, 3, 1, 4, 5)
    flat_rows = result.reshape(row_count * column_count, model_width)
    return flat_rows.reshape(row_count, column_count, model_width)


def solution(mesh):
    placed = (P("lat", "lon", None), P(), P())
    return jax.shard_map(
        body, mesh=mesh, in_specs=placed, out_specs=P("lat", "lon", None), check_vma=False
    )
```

profile of v0, /device:TPU:0, one launch (start us, length us, event | category | flops | bytes accessed | tf_op | source)
XLA Modules:
  0.0 296.9 jit_solution(6816487896089749066)
XLA Ops:
  0.0 0.0 copy-start
  0.0 41.6 %all_to_all.10 = bf16[128,1,1,32,256]{4,3,2,1,0:T(8,128)(2,1)S(1)} all-to-all(bf16[128,1,1,32,256]{4,3,2,1,0:T(8,128)(2,1)} %bitcast.57), channel_id=1, replica_groups=mesh['lat'=16,'lon'=8] {'lat','lon'}, dimensions={0} | all-to-all | bytes 4194304 | tf_op jit(solution)/shard_map/all_to_all | solution.py:64
  41.6 0.0 copy-done
  41.6 4.5 %convolution_convert_fusion = bf16[4096,768]{1,0:T(8,128)(2,1)} fusion(bf16[4096,256]{1,0:T(8,128)(2,1)S(1)} %bitcast.55, bf16[256,768]{1,0:T(8,128)(2,1)S(1)} %copy-done), kind=kOutput, calls=%fused_computation.11 | convolution fusion | flops 1613758464 | bytes 8781824 | tf_op jit(solution)/shard_map/dot_general | solution.py:16
  46.1 28.4 %reshape.38 = bf16[8,2,8,1,1,32,3,8,32]{8,7,6,5,2,1,0,4,3:T(8,128)(2,1)} reshape(bf16[4096,768]{1,0:T(8,128)(2,1)} %convolution_convert_fusion) | data formatting | bytes 12582912 | tf_op jit(solution)/shard_map/reshape | solution.py:19
  74.5 16.8 %fusion.5 = (bf16[8,2,8,1,1,32,1,8,32]{8,7,6,5,2,1,0,4,3:T(8,128)(2,1)}, bf16[8,2,8,1,1,32,1,8,32]{8,7,6,5,2,1,0,4,3:T(8,128)(2,1)}, bf16[8,2,8,1,1,32,1,8,32]{8,7,6,5,2,1,0,4,3:T(8,128)(2,1)}) fusion(bf16[8,2,8,1,1,32,3,8,32]{8,7,6,5,2,1,0,4,3:T(8,128)(2,1)} %reshape.38), kind=kLoop, calls=%fused_computation.14 | loop fusion | bytes 12582912 | tf_op jit(solution)/shard_map/slice | solution.py:22
  91.3 54.6 %multiply_reduce_fusion = (f32[2,32,8,8,8]{4,3,2,1,0:T(8,128)S(1)}, f32[2,32,8,8,8,8,8]{4,6,5,3,2,1,0:T(8,128)}) fusion(bf16[8,2,8,1,1,32,1,8,32]{8,7,6,5,2,1,0,4,3:T(8,128)(2,1)} %get-tuple-element.7, bf16[8,2,8,1,1,32,1,8,32]{8,7,6,5,2,1,0,4,3:T(8,128)(2,1)} %get-tuple-element.6), kind=kOutput, calls=%fused_computation.2 | convolution fusion | flops 138379264 | bytes 12713984 | tf_op jit(solution)/shard_map/gsjnlche,xsynzche->snchgjlxyz/dot_general | solution.py:29
  146.0 42.7 %fusion = f32[2,32,8,8,8]{4,3,2,1,0:T(8,128)} fusion(f32[2,32,8,8,8,8,8]{4,6,5,3,2,1,0:T(8,128)} %get-tuple-element.9, f32[2,32,8,8,8]{4,3,2,1,0:T(8,128)S(1)} %get-tuple-element.8), kind=kLoop, calls=%fused_computation.3 | loop fusion | flops 6258688 | bytes 8650752 | tf_op jit(solution)/shard_map/reduce_sum | solution.py:40
  188.7 50.0 %fusion.2 = bf16[8,2,8,1,1,32,8,32]{7,2,0,6,5,1,4,3:T(8,128)(2,1)} fusion(f32[2,32,8,8,8,8,8]{4,6,5,3,2,1,0:T(8,128)} %get-tuple-element.9, f32[2,32,8,8,8]{4,3,2,1,0:T(8,128)} %fusion, f32[2,32,8,8,8]{4,3,2,1,0:T(8,128)S(1)} %get-tuple-element.8, bf16[8,2,8,1,1,32,1,8,32]{8,7,6,5,2,1,0,4,3:T(8,128)(2,1)} %get-tuple-element.5), kind=kOutput, calls=%fused_computation.6 | convolution fusion | flops 143654912 | bytes 12845056 | tf_op jit(solution)/shard_map/snchgjlxyz,xsynzche->gsjnlche/dot_general | solution.py:41
  238.7 12.0 %copy.17 = bf16[8,2,8,1,1,32,8,32]{7,6,5,2,1,0,4,3:T(8,128)(2,1)} copy(bf16[8,2,8,1,1,32,8,32]{7,2,0,6,5,1,4,3:T(8,128)(2,1)} %fusion.2) | data formatting | bytes 4194304 | tf_op jit(solution)/shard_map/convert_element_type | solution.py:46
  250.7 0.0 copy-start.2
  250.7 0.0 copy-start.1
  250.7 9.8 %reshape.42 = bf16[4096,256]{1,0:T(8,128)(2,1)S(1)} reshape(bf16[8,2,8,1,1,32,8,32]{7,6,5,2,1,0,4,3:T(8,128)(2,1)} %copy.17) | data formatting | bytes 4194304 | tf_op jit(solution)/shard_map/reshape | solution.py:47
  260.5 0.0 copy-done.2
  260.5 0.7 convolution_convert_fusion.1
  261.2 34.4 %all_to_all.11 = bf16[128,1,1,32,256]{4,3,2,1,0:T(8,128)(2,1)S(1)} all-to-all(bf16[128,1,1,32,256]{4,3,2,1,0:T(8,128)(2,1)S(1)} %bitcast.54), channel_id=1, replica_groups=mesh['lat'=16,'lon'=8] {'lat','lon'}, dimensions={0} | all-to-all | bytes 4194304 | tf_op jit(solution)/shard_map/all_to_all | solution.py:73
  295.6 1.3 copy.41
  296.9 0.0 copy-done.1
Async XLA Ops:
  0.0 41.6 %copy-start = (bf16[256,768]{1,0:T(8,128)(2,1)S(1)}, bf16[256,768]{1,0:T(8,128)(2,1)}, u32[]{:S(2)}) copy-start(bf16[256,768]{1,0:T(8,128)(2,1)} %param.4) | copy-start | bytes 1179652
  250.7 9.8 %copy-start.2 = (bf16[256,256]{1,0:T(8,128)(2,1)S(1)}, bf16[256,256]{1,0:T(8,128)(2,1)}, u32[]{:S(2)}) copy-start(bf16[256,256]{1,0:T(8,128)(2,1)} %param.5) | copy-start | bytes 393220
  250.7 46.3 %copy-start.1 = (bf16[256,768]{1,0:T(8,128)(2,1)S(1)}, bf16[256,768]{1,0:T(8,128)(2,1)}, u32[]{:S(2)}) copy-start(bf16[256,768]{1,0:T(8,128)(2,1)} %param.4) | copy-start | bytes 1179652
where the time goes:
time: 298 us; the launch traced here: 297 us
  matrix products  110 us (37%)
  blocking collectives  76 us (26%)
  local copies, waits for them, and re-layouts  68.4 us (23%)
  other arithmetic  42.7 us (14%)
    dot_general x1, matrix products, attend(): jnp.einsum(layout + 'he,' + partner + 'he->' + groups + 'h' + members + k...  54.6 us
    dot_general x1, matrix products, attend(): jnp.einsum(groups + 'h' + members + keyset + ',' + partner + 'he->' + lay...  50 us
    reduce_sum x1, other arithmetic, attend(): jnp.sum(exponent, axis=sum_axes, keepdims=True)  42.7 us
    all_to_all x1, blocking collectives, body(): lax.all_to_all(ordered, ('lat', 'lon'), split_axis=0, concat_axis=0, tile...  41.6 us
    all_to_all x1, blocking collectives, body(): lax.all_to_all(processed, ('lat', 'lon'), split_axis=0, concat_axis=0, ti...  34.4 us
    reshape x1, local copies, waits for them, and re-layouts, attend(): qkv = qkv.reshape(lead_shape + (3, HEADS, head_size))  28.4 us
    slice x1, local copies, waits for them, and re-layouts, attend(): value_part = qkv[..., 2, :, :]  16.8 us
    convert_element_type x1, local copies, waits for them, and re-layouts, attend(): mixed = jnp.einsum(groups + 'h' + members + keyset + ',' + partner + 'he-...  12 us

commit v1 on v0

v1 whole, which is shorter than its diff:
```python
import functools
import math

import jax
import jax.numpy as jnp
import numpy as np
from jax import lax
from jax.experimental import pallas as pl
from jax.experimental.pallas import tpu as pltpu
from jax.sharding import PartitionSpec as P

HEADS = 8
GRID = 8
LANES = 128
F32 = jnp.float32
BF16 = jnp.bfloat16


def member_order(lat_count, lon_count):
    share = lat_count // GRID
    index = np.arange(lat_count * lon_count).reshape(4, 2, share, 2, lon_count // 2)
    index = index.transpose(2, 0, 1, 3, 4).reshape(share, 4, 4, lon_count // 2)
    lists = []
    for which in range(share):
        order = (2, 1, 0) if which % 2 == 0 else (0, 1, 2)
        lists.append(index[which].transpose(order).reshape(-1).tolist())
    return lists


def attend_half(query, key, value, masks, scale):
    members = query.shape[0]
    spread = jnp.concatenate([query * mask for mask in masks], axis=0)
    scores = lax.dot_general(key, spread, (((1,), (1,)), ((), ())), preferred_element_type=F32) * scale
    exponent = jnp.exp(scores - jnp.max(scores, axis=0, keepdims=True))
    total = jnp.sum(exponent, axis=0, keepdims=True)
    weights = (exponent * (1.0 / total)).astype(BF16)
    product = lax.dot_general(weights, value, (((0,), (0,)), ((), ())), preferred_element_type=F32)
    mixed = None
    for head, mask in enumerate(masks):
        term = product[head * members : (head + 1) * members] * mask.astype(F32)
        mixed = term if mixed is None else mixed + term
    return mixed.astype(BF16)


def attend_kernel(members, groups, unroll, tokens, w_qkv, w_out, out, *scratch):
    width = tokens.shape[-1]
    halves = width // LANES
    head_size = width // HEADS
    scale = 1.0 / math.sqrt(head_size)
    arrived, finished = scratch[:halves], scratch[halves:]
    for half in range(halves):
        part = tokens[:, :, half * LANES : (half + 1) * LANES]
        arrived[half][...] = part.reshape(members * groups, LANES).astype(F32)
    lane = lax.broadcasted_iota(jnp.int32, (1, LANES), 1)
    masks = [
        ((lane >= first) & (lane < first + head_size)).astype(F32).astype(BF16)
        for first in range(0, LANES, head_size)
    ]

    def step(index, carry):
        blocks = []
        for at in range(unroll):
            rows = pl.ds(index * unroll + at, members, stride=groups)
            blocks.append(jnp.concatenate([ref[rows, :].astype(BF16) for ref in arrived], axis=1))
        block = jnp.concatenate(blocks, axis=0)
        qkv = jnp.dot(block, w_qkv[...], preferred_element_type=F32).astype(BF16)
        mixed = []
        for at in range(unroll):
            rows = slice(at * members, (at + 1) * members)
            parts = []
            for half in range(halves):
                columns = [
                    slice(kind * width + half * LANES, kind * width + (half + 1) * LANES) for kind in range(3)
                ]
                parts.append(attend_half(*[qkv[rows, column] for column in columns], masks, scale))
            mixed.append(jnp.concatenate(parts, axis=1))
        result = jnp.dot(jnp.concatenate(mixed, axis=0), w_out[...], preferred_element_type=F32)
        for at in range(unroll):
            rows = pl.ds(index * unroll + at, members, stride=groups)
            for half in range(halves):
                finished[half][rows, :] = result[
                    at * members : (at + 1) * members, half * LANES : (half + 1) * LANES
                ]
        return carry

    lax.fori_loop(0, groups // unroll, step, 0)
    for half in range(halves):
        part = finished[half][...].astype(BF16).reshape(members, groups, LANES)
        out[:, :, half * LANES : (half + 1) * LANES] = part


def attend(tokens, w_qkv, w_out):
    members, groups, width = tokens.shape
    vmem = pl.BlockSpec(memory_space=pltpu.VMEM)
    return pl.pallas_call(
        functools.partial(attend_kernel, members, groups, 4),
        out_shape=jax.ShapeDtypeStruct(tokens.shape, BF16),
        in_specs=[vmem] * 3,
        out_specs=vmem,
        scratch_shapes=[pltpu.VMEM((members * groups, LANES), F32)] * (2 * width // LANES),
        compiler_params=pltpu.CompilerParams(vmem_limit_bytes=40 * 1024 * 1024),
    )(tokens, w_qkv, w_out)


def body(lists, tokens, w_qkv, w_out):
    rows, columns, width = tokens.shape
    members = len(lists[0])
    exchange = functools.partial(
        lax.all_to_all,
        axis_name=("lat", "lon"),
        split_axis=0,
        concat_axis=0,
        axis_index_groups=lists,
        tiled=True,
    )
    arrived = exchange(tokens.reshape(members, rows * columns // members, width))
    returned = exchange(attend(arrived, w_qkv, w_out))
    return returned.reshape(rows, columns, width)


def solution(mesh):
    lists = member_order(mesh.shape["lat"], mesh.shape["lon"])
    placed = (P("lat", "lon", None), P(), P())
    return jax.shard_map(
        functools.partial(body, lists),
        mesh=mesh,
        in_specs=placed,
        out_specs=P("lat", "lon", None),
        check_vma=False,
    )
```

time: 298 us -> 99.5 us (0.33)
  matrix products: 110 us -> 0 us
  local copies, waits for them, and re-layouts: 68.4 us -> 1.33 us
  other arithmetic: 42.7 us -> 0 us
  Pallas kernels: 0 us -> 22.4 us
    dot_general x4 -> x0, matrix products: 110 us -> none  [the longest x1 54.6 us: attend(): jnp.einsum(layout + 'he,' + partner + 'he->' + groups + 'h' + members + k...]
    reduce_sum x1 -> x0, other arithmetic: 42.7 us -> none  [attend(): jnp.sum(exponent, axis=sum_axes, keepdims=True)]
    reshape x2 -> x0, local copies, waits for them, and re-layouts: 38.2 us -> none  [the longest x1 28.4 us: attend(): qkv = qkv.reshape(lead_shape + (3, HEADS, head_size))]
    pallas_call x0 -> x1, Pallas kernels: none -> 22.4 us  [attend(): pl.pallas_call(functools.partial(attend_kernel, members, groups, 4), out_...]
    slice x1 -> x0, local copies, waits for them, and re-layouts: 16.8 us -> none  [attend(): value_part = qkv[..., 2, :, :]]
    convert_element_type x1 -> x0, local copies, waits for them, and re-layouts: 12 us -> none  [attend(): mixed = jnp.einsum(groups + 'h' + members + keyset + ',' + partner + 'he-...]
where the time goes in v1:
time: 99.5 us; the launch traced here: 99.2 us
  blocking collectives  75.5 us (76%)
  Pallas kernels  22.4 us (23%)
  local copies, waits for them, and re-layouts  1.33 us (1%)
    all_to_all x1, blocking collectives, body(): exchange(tokens.reshape(members, rows * columns // members, width))  41.6 us
    all_to_all x1, blocking collectives, body(): returned = exchange(attend(arrived, w_qkv, w_out))  33.9 us
    pallas_call x1, Pallas kernels, attend(): pl.pallas_call(functools.partial(attend_kernel, members, groups, 4), out_...  22.4 us

profile of v1, /device:TPU:0, one launch (start us, length us, event | category | flops | bytes accessed | tf_op | source)
XLA Modules:
  0.0 99.2 jit_solution(13538203366427700463)
XLA Ops:
  0.0 0.0 copy-start
  0.0 0.0 copy-start.1
  0.0 41.6 %all_to_all.10.tokens = bf16[64,64,256]{2,1,0:T(8,128)(2,1)S(1)} all-to-all(bf16[64,64,256]{2,1,0:T(8,128)(2,1)} %bitcast.3), channel_id=1, replica_groups={{0,32,64,96,4,36,68,100,16,48,80,112,20,52,84,116,1,33,65,97,5,37,69,10..., dimensions={0} | all-to-all | bytes 4194304 | tf_op jit(solution)/shard_map/all_to_all | solution.py:116
  41.6 0.0 copy-done
  41.6 0.0 copy-done.1
  41.6 22.4 %shard_map.37 = bf16[64,64,256]{2,1,0:T(8,128)(2,1)S(1)} custom-call(bf16[64,64,256]{2,1,0:T(8,128)(2,1)S(1)} %all_to_all.10.tokens, bf16[256,768]{1,0:T(8,128)(2,1)S(1)} %copy-done, bf16[256,256]{1,0:T(8,128)(2,1)S(1)} %copy-done.1), custom_call_target="tpu_custom_call" | custom-call | tf_op jit(solution)/shard_map/pallas_call | solution.py:95
  64.0 33.9 %all_to_all.11 = bf16[64,64,256]{2,1,0:T(8,128)(2,1)S(1)} all-to-all(bf16[64,64,256]{2,1,0:T(8,128)(2,1)S(1)} %shard_map.37), channel_id=1, replica_groups={{0,32,64,96,4,36,68,100,16,48,80,112,20,52,84,116,1,33,65,97,5,37,69,10..., dimensions={0} | all-to-all | bytes 4194304 | tf_op jit(solution)/shard_map/all_to_all | solution.py:117
  97.9 1.3 %copy.5 = bf16[16,256,256]{2,1,0:T(8,128)(2,1)} copy(bf16[16,256,256]{2,1,0:T(8,128)(2,1)S(1)} %bitcast.2) | data formatting | bytes 4194304
Async XLA Ops:
  0.0 41.6 %copy-start = (bf16[256,768]{1,0:T(8,128)(2,1)S(1)}, bf16[256,768]{1,0:T(8,128)(2,1)}, u32[]{:S(2)}) copy-start(bf16[256,768]{1,0:T(8,128)(2,1)} %w_qkv.1) | copy-start | bytes 1179652
  0.0 41.6 %copy-start.1 = (bf16[256,256]{1,0:T(8,128)(2,1)S(1)}, bf16[256,256]{1,0:T(8,128)(2,1)}, u32[]{:S(2)}) copy-start(bf16[256,256]{1,0:T(8,128)(2,1)} %w_out.1) | copy-start | bytes 393220

commit v2 on v1

v2 whole, which is shorter than its diff:
```python
import functools
import math

import jax
import jax.numpy as jnp
import numpy as np
from jax import lax
from jax.experimental import pallas as pl
from jax.experimental.pallas import tpu as pltpu
from jax.sharding import PartitionSpec as P

HEADS = 8
GRID = 8
LANES = 128
F32 = jnp.float32
BF16 = jnp.bfloat16


def member_order(lat_count, lon_count):
    share = lat_count // GRID
    index = np.arange(lat_count * lon_count).reshape(4, 2, share, 2, lon_count // 2)
    index = index.transpose(2, 0, 1, 3, 4).reshape(share, 4, 4, lon_count // 2)
    lists = []
    for which in range(share):
        order = (2, 1, 0) if which % 2 == 0 else (0, 1, 2)
        lists.append(index[which].transpose(order).reshape(-1).tolist())
    return lists


def attend_scores(query, key, masks):
    spread = jnp.concatenate([key * mask for mask in masks], axis=0)
    return lax.dot_general(query, spread, (((1,), (1,)), ((), ())), preferred_element_type=F32)


def exponentials(scores, factor):
    first = lax.broadcasted_iota(jnp.int32, (scores.shape[0], LANES), 1) < LANES // 2
    tiles = []
    for at in range(0, scores.shape[1], LANES):
        tile = scores[:, at : at + LANES]
        low = jnp.max(jnp.where(first, tile, -jnp.inf), axis=1, keepdims=True)
        high = jnp.max(jnp.where(first, -jnp.inf, tile), axis=1, keepdims=True)
        tiles.append(jnp.exp2((tile - jnp.where(first, low, high)) * factor).astype(BF16))
    return jnp.concatenate(tiles, axis=1)


def mix_values(exponent, value, masks, ones):
    spread = jnp.concatenate([value * mask for mask in masks], axis=0)
    both = jnp.dot(exponent, jnp.concatenate([spread, ones], axis=1), preferred_element_type=F32)
    return (both[:, :LANES] * (1.0 / both[:, LANES:])).astype(BF16)


def attend_kernel(members, groups, unroll, pitch, tokens, w_qkv, w_out, out, *scratch):
    width = tokens.shape[-1]
    halves = width // LANES
    head_size = width // HEADS
    factor = math.log2(math.e) / math.sqrt(head_size)
    arrived, finished = scratch[:halves], scratch[halves:]
    for half in range(halves):
        for member in range(members):
            part = tokens[member, :, half * LANES : (half + 1) * LANES]
            arrived[half][member * pitch : member * pitch + groups, :] = part.astype(F32)
    lane = lax.broadcasted_iota(jnp.int32, (1, LANES), 1)
    masks = [
        ((lane >= first) & (lane < first + head_size)).astype(F32).astype(BF16)
        for first in range(0, LANES, head_size)
    ]
    ones = jnp.concatenate([jnp.broadcast_to(mask, (members, LANES)) for mask in masks], axis=0)

    def step(index, carry):
        blocks = []
        for at in range(unroll):
            rows = pl.ds(index * unroll + at, members, stride=pitch)
            blocks.append(jnp.concatenate([ref[rows, :].astype(BF16) for ref in arrived], axis=1))
        block = jnp.concatenate(blocks, axis=0)
        qkv = jnp.dot(block, w_qkv[...], preferred_element_type=F32).astype(BF16)
        cells = [(at, half) for at in range(unroll) for half in range(halves)]

        def piece(cell, kind):
            at, half = cell
            left = kind * width + half * LANES
            return qkv[at * members : (at + 1) * members, left : left + LANES]

        scores = [attend_scores(piece(cell, 0), piece(cell, 1), masks) for cell in cells]
        exponents = [exponentials(score, factor) for score in scores]
        mixed = [mix_values(exponents[n], piece(cell, 2), masks, ones) for n, cell in enumerate(cells)]
        joined = [jnp.concatenate(mixed[n : n + halves], axis=1) for n in range(0, len(mixed), halves)]
        result = jnp.dot(jnp.concatenate(joined, axis=0), w_out[...], preferred_element_type=F32)
        for at in range(unroll):
            rows = pl.ds(index * unroll + at, members, stride=pitch)
            for half in range(halves):
                finished[half][rows, :] = result[
                    at * members : (at + 1) * members, half * LANES : (half + 1) * LANES
                ]
        return carry

    lax.fori_loop(0, groups // unroll, step, 0)
    for half in range(halves):
        for member in range(members):
            part = finished[half][member * pitch : member * pitch + groups, :].astype(BF16)
            out[member, :, half * LANES : (half + 1) * LANES] = part


def attend(tokens, w_qkv, w_out):
    members, groups, width = tokens.shape
    pitch = groups + 8
    vmem = pl.BlockSpec(memory_space=pltpu.VMEM)
    return pl.pallas_call(
        functools.partial(attend_kernel, members, groups, 16, pitch),
        out_shape=jax.ShapeDtypeStruct(tokens.shape, BF16),
        in_specs=[vmem] * 3,
        out_specs=vmem,
        scratch_shapes=[pltpu.VMEM((members * pitch, LANES), F32)] * (2 * width // LANES),
        compiler_params=pltpu.CompilerParams(vmem_limit_bytes=40 * 1024 * 1024),
    )(tokens, w_qkv, w_out)


def body(lists, tokens, w_qkv, w_out):
    rows, columns, width = tokens.shape
    members = len(lists[0])
    exchange = functools.partial(
        lax.all_to_all,
        axis_name=("lat", "lon"),
        split_axis=0,
        concat_axis=0,
        axis_index_groups=lists,
        tiled=True,
    )
    arrived = exchange(tokens.reshape(members, rows * columns // members, width))
    returned = exchange(attend(arrived, w_qkv, w_out))
    return returned.reshape(rows, columns, width)


def solution(mesh):
    lists = member_order(mesh.shape["lat"], mesh.shape["lon"])
    placed = (P("lat", "lon", None), P(), P())
    return jax.shard_map(
        functools.partial(body, lists),
        mesh=mesh,
        in_specs=placed,
        out_specs=P("lat", "lon", None),
        check_vma=False,
    )
```

time: 99.5 us -> 86 us (0.86)
  Pallas kernels: 22.4 us -> 8.91 us
    pallas_call x1, Pallas kernels: 22.4 us -> 8.91 us  [attend(): pl.pallas_call(functools.partial(attend_kernel, members, groups, 16, pitc...]
where the time goes in v2:
time: 86 us; the launch traced here: 85.7 us
  blocking collectives  75.5 us (88%)
  Pallas kernels  8.91 us (10%)
  local copies, waits for them, and re-layouts  1.33 us (2%)
    all_to_all x1, blocking collectives, body(): exchange(tokens.reshape(members, rows * columns // members, width))  41.6 us
    all_to_all x1, blocking collectives, body(): returned = exchange(attend(arrived, w_qkv, w_out))  33.9 us
    pallas_call x1, Pallas kernels, attend(): pl.pallas_call(functools.partial(attend_kernel, members, groups, 16, pitc...  8.91 us

profile of v2, /device:TPU:0, one launch (start us, length us, event | category | flops | bytes accessed | tf_op | source)
XLA Modules:
  0.0 85.7 jit_solution(3626253502267991463)
XLA Ops:
  0.0 0.0 copy-start
  0.0 0.0 copy-start.1
  0.0 41.6 %all_to_all.10.tokens = bf16[64,64,256]{2,1,0:T(8,128)(2,1)S(1)} all-to-all(bf16[64,64,256]{2,1,0:T(8,128)(2,1)} %bitcast.3), channel_id=1, replica_groups={{0,32,64,96,4,36,68,100,16,48,80,112,20,52,84,116,1,33,65,97,5,37,69,10..., dimensions={0} | all-to-all | bytes 4194304 | tf_op jit(solution)/shard_map/all_to_all | solution.py:128
  41.6 0.0 copy-done
  41.6 0.0 copy-done.1
  41.6 8.9 %shard_map.37 = bf16[64,64,256]{2,1,0:T(8,128)(2,1)S(1)} custom-call(bf16[64,64,256]{2,1,0:T(8,128)(2,1)S(1)} %all_to_all.10.tokens, bf16[256,768]{1,0:T(8,128)(2,1)S(1)} %copy-done, bf16[256,256]{1,0:T(8,128)(2,1)S(1)} %copy-done.1), custom_call_target="tpu_custom_call" | custom-call | tf_op jit(solution)/shard_map/pallas_call | solution.py:107
  50.5 33.9 %all_to_all.11 = bf16[64,64,256]{2,1,0:T(8,128)(2,1)S(1)} all-to-all(bf16[64,64,256]{2,1,0:T(8,128)(2,1)S(1)} %shard_map.37), channel_id=1, replica_groups={{0,32,64,96,4,36,68,100,16,48,80,112,20,52,84,116,1,33,65,97,5,37,69,10..., dimensions={0} | all-to-all | bytes 4194304 | tf_op jit(solution)/shard_map/all_to_all | solution.py:129
  84.4 1.3 %copy.5 = bf16[16,256,256]{2,1,0:T(8,128)(2,1)} copy(bf16[16,256,256]{2,1,0:T(8,128)(2,1)S(1)} %bitcast.2) | data formatting | bytes 4194304
Async XLA Ops:
  0.0 41.6 %copy-start = (bf16[256,768]{1,0:T(8,128)(2,1)S(1)}, bf16[256,768]{1,0:T(8,128)(2,1)}, u32[]{:S(2)}) copy-start(bf16[256,768]{1,0:T(8,128)(2,1)} %w_qkv.1) | copy-start | bytes 1179652
  0.0 41.6 %copy-start.1 = (bf16[256,256]{1,0:T(8,128)(2,1)S(1)}, bf16[256,256]{1,0:T(8,128)(2,1)}, u32[]{:S(2)}) copy-start(bf16[256,256]{1,0:T(8,128)(2,1)} %w_out.1) | copy-start | bytes 393220

commit v3 on v2

--- a/solution.py
+++ b/solution.py
@@ -20,11 +20,7 @@
     share = lat_count // GRID
     index = np.arange(lat_count * lon_count).reshape(4, 2, share, 2, lon_count // 2)
     index = index.transpose(2, 0, 1, 3, 4).reshape(share, 4, 4, lon_count // 2)
-    lists = []
-    for which in range(share):
-        order = (2, 1, 0) if which % 2 == 0 else (0, 1, 2)
-        lists.append(index[which].transpose(order).reshape(-1).tolist())
-    return lists
+    return index.transpose(0, 3, 1, 2).reshape(share, -1).tolist()
 
 
 def attend_scores(query, key, masks):
@@ -105,7 +101,7 @@
     pitch = groups + 8
     vmem = pl.BlockSpec(memory_space=pltpu.VMEM)
     return pl.pallas_call(
-        functools.partial(attend_kernel, members, groups, 16, pitch),
+        functools.partial(attend_kernel, members, groups, groups, pitch),
         out_shape=jax.ShapeDtypeStruct(tokens.shape, BF16),
         in_specs=[vmem] * 3,
         out_specs=vmem,

time: 86 us -> 84.6 us (0.984)
  no operation moved by 1% of the time
where the time goes in v3:
time: 84.6 us; the launch traced here: 84.4 us
  blocking collectives  74.9 us (89%)
  Pallas kernels  8.13 us (10%)
  local copies, waits for them, and re-layouts  1.33 us (2%)
    all_to_all x1, blocking collectives, body(): exchange(tokens.reshape(members, rows * columns // members, width))  41.2 us
    all_to_all x1, blocking collectives, body(): returned = exchange(attend(arrived, w_qkv, w_out))  33.7 us
    pallas_call x1, Pallas kernels, attend(): pl.pallas_call(functools.partial(attend_kernel, members, groups, groups,...  8.13 us

profile of v3, /device:TPU:0, one launch (start us, length us, event | category | flops | bytes accessed | tf_op | source)
XLA Modules:
  0.0 84.4 jit_solution(17847855520964029688)
XLA Ops:
  0.0 0.0 copy-start
  0.0 0.0 copy-start.1
  0.0 41.2 %all_to_all.10.tokens = bf16[64,64,256]{2,1,0:T(8,128)(2,1)S(1)} all-to-all(bf16[64,64,256]{2,1,0:T(8,128)(2,1)} %bitcast.3), channel_id=1, replica_groups={{0,4,16,20,32,36,48,52,64,68,80,84,96,100,112,116,1,5,17,21,33,37,49,53..., dimensions={0} | all-to-all | bytes 4194304 | tf_op jit(solution)/shard_map/all_to_all | solution.py:124
  41.2 0.0 copy-done
  41.2 0.0 copy-done.1
  41.2 8.1 %shard_map.37 = bf16[64,64,256]{2,1,0:T(8,128)(2,1)S(1)} custom-call(bf16[64,64,256]{2,1,0:T(8,128)(2,1)S(1)} %all_to_all.10.tokens, bf16[256,768]{1,0:T(8,128)(2,1)S(1)} %copy-done, bf16[256,256]{1,0:T(8,128)(2,1)S(1)} %copy-done.1), custom_call_target="tpu_custom_call" | custom-call | tf_op jit(solution)/shard_map/pallas_call | solution.py:103
  49.4 33.7 %all_to_all.11 = bf16[64,64,256]{2,1,0:T(8,128)(2,1)S(1)} all-to-all(bf16[64,64,256]{2,1,0:T(8,128)(2,1)S(1)} %shard_map.37), channel_id=1, replica_groups={{0,4,16,20,32,36,48,52,64,68,80,84,96,100,112,116,1,5,17,21,33,37,49,53..., dimensions={0} | all-to-all | bytes 4194304 | tf_op jit(solution)/shard_map/all_to_all | solution.py:125
  83.1 1.3 %copy.5 = bf16[16,256,256]{2,1,0:T(8,128)(2,1)} copy(bf16[16,256,256]{2,1,0:T(8,128)(2,1)S(1)} %bitcast.2) | data formatting | bytes 4194304
Async XLA Ops:
  0.0 41.2 %copy-start = (bf16[256,768]{1,0:T(8,128)(2,1)S(1)}, bf16[256,768]{1,0:T(8,128)(2,1)}, u32[]{:S(2)}) copy-start(bf16[256,768]{1,0:T(8,128)(2,1)} %w_qkv.1) | copy-start | bytes 1179652
  0.0 41.2 %copy-start.1 = (bf16[256,256]{1,0:T(8,128)(2,1)S(1)}, bf16[256,256]{1,0:T(8,128)(2,1)}, u32[]{:S(2)}) copy-start(bf16[256,256]{1,0:T(8,128)(2,1)} %w_out.1) | copy-start | bytes 393220

commit v4 on v3

--- a/solution.py
+++ b/solution.py
@@ -20,7 +20,11 @@
     share = lat_count // GRID
     index = np.arange(lat_count * lon_count).reshape(4, 2, share, 2, lon_count // 2)
     index = index.transpose(2, 0, 1, 3, 4).reshape(share, 4, 4, lon_count // 2)
-    return index.transpose(0, 3, 1, 2).reshape(share, -1).tolist()
+    lists = []
+    for which in range(share):
+        chips = np.roll(index[which], 2 * which, (0, 1, 2))
+        lists.append(chips.transpose(2, 0, 1).reshape(-1).tolist())
+    return lists
 
 
 def attend_scores(query, key, masks):

time: 84.6 us -> 82.2 us (0.972)
  blocking collectives: 74.9 us -> 72.5 us
    all_to_all x1, blocking collectives: 41.2 us -> 38.7 us  [body(): exchange(tokens.reshape(members, rows * columns // members, width))]
where the time goes in v4:
time: 82.2 us; the launch traced here: 81.9 us
  blocking collectives  72.5 us (88%)
  Pallas kernels  8.13 us (10%)
  local copies, waits for them, and re-layouts  1.33 us (2%)
    all_to_all x1, blocking collectives, body(): exchange(tokens.reshape(members, rows * columns // members, width))  38.7 us
    all_to_all x1, blocking collectives, body(): returned = exchange(attend(arrived, w_qkv, w_out))  33.8 us
    pallas_call x1, Pallas kernels, attend(): pl.pallas_call(functools.partial(attend_kernel, members, groups, groups,...  8.13 us

profile of v4, /device:TPU:0, one launch (start us, length us, event | category | flops | bytes accessed | tf_op | source)
XLA Modules:
  0.0 81.9 jit_solution(14063771986143526178)
XLA Ops:
  0.0 0.0 copy-start
  0.0 0.0 copy-start.1
  0.0 38.7 %all_to_all.10.tokens = bf16[64,64,256]{2,1,0:T(8,128)(2,1)S(1)} all-to-all(bf16[64,64,256]{2,1,0:T(8,128)(2,1)} %bitcast.3), channel_id=1, replica_groups={{0,4,16,20,32,36,48,52,64,68,80,84,96,100,112,116,1,5,17,21,33,37,49,53..., dimensions={0} | all-to-all | bytes 4194304 | tf_op jit(solution)/shard_map/all_to_all | solution.py:128
  38.7 0.0 copy-done
  38.7 0.0 copy-done.1
  38.7 8.1 %shard_map.37 = bf16[64,64,256]{2,1,0:T(8,128)(2,1)S(1)} custom-call(bf16[64,64,256]{2,1,0:T(8,128)(2,1)S(1)} %all_to_all.10.tokens, bf16[256,768]{1,0:T(8,128)(2,1)S(1)} %copy-done, bf16[256,256]{1,0:T(8,128)(2,1)S(1)} %copy-done.1), custom_call_target="tpu_custom_call" | custom-call | tf_op jit(solution)/shard_map/pallas_call | solution.py:107
  46.9 33.8 %all_to_all.11 = bf16[64,64,256]{2,1,0:T(8,128)(2,1)S(1)} all-to-all(bf16[64,64,256]{2,1,0:T(8,128)(2,1)S(1)} %shard_map.37), channel_id=1, replica_groups={{0,4,16,20,32,36,48,52,64,68,80,84,96,100,112,116,1,5,17,21,33,37,49,53..., dimensions={0} | all-to-all | bytes 4194304 | tf_op jit(solution)/shard_map/all_to_all | solution.py:129
  80.6 1.3 %copy.5 = bf16[16,256,256]{2,1,0:T(8,128)(2,1)} copy(bf16[16,256,256]{2,1,0:T(8,128)(2,1)S(1)} %bitcast.2) | data formatting | bytes 4194304
Async XLA Ops:
  0.0 38.7 %copy-start = (bf16[256,768]{1,0:T(8,128)(2,1)S(1)}, bf16[256,768]{1,0:T(8,128)(2,1)}, u32[]{:S(2)}) copy-start(bf16[256,768]{1,0:T(8,128)(2,1)} %w_qkv.1) | copy-start | bytes 1179652
  0.0 38.7 %copy-start.1 = (bf16[256,256]{1,0:T(8,128)(2,1)S(1)}, bf16[256,256]{1,0:T(8,128)(2,1)}, u32[]{:S(2)}) copy-start(bf16[256,256]{1,0:T(8,128)(2,1)} %w_out.1) | copy-start | bytes 393220

commit v5 on v4

--- a/solution.py
+++ b/solution.py
@@ -23,7 +23,7 @@
     lists = []
     for which in range(share):
         chips = np.roll(index[which], 2 * which, (0, 1, 2))
-        lists.append(chips.transpose(2, 0, 1).reshape(-1).tolist())
+        lists.append(chips.transpose(0, 2, 1).reshape(-1).tolist())
     return lists
 
 

time: 82.2 us -> 81.1 us (0.987)
  blocking collectives: 72.5 us -> 71.1 us
    all_to_all x1, blocking collectives: 38.7 us -> 37.2 us  [body(): exchange(tokens.reshape(members, rows * columns // members, width))]
where the time goes in v5:
time: 81.1 us; the launch traced here: 80.6 us
  blocking collectives  71.1 us (88%)
  Pallas kernels  8.14 us (10%)
  local copies, waits for them, and re-layouts  1.33 us (2%)
    all_to_all x1, blocking collectives, body(): exchange(tokens.reshape(members, rows * columns // members, width))  37.2 us
    all_to_all x1, blocking collectives, body(): returned = exchange(attend(arrived, w_qkv, w_out))  33.9 us
    pallas_call x1, Pallas kernels, attend(): pl.pallas_call(functools.partial(attend_kernel, members, groups, groups,...  8.14 us

profile of v5, /device:TPU:0, one launch (start us, length us, event | category | flops | bytes accessed | tf_op | source)
XLA Modules:
  0.0 80.6 jit_solution(3165896122775797354)
XLA Ops:
  0.0 0.0 copy-start
  0.0 0.0 copy-start.1
  0.0 37.2 %all_to_all.10.tokens = bf16[64,64,256]{2,1,0:T(8,128)(2,1)S(1)} all-to-all(bf16[64,64,256]{2,1,0:T(8,128)(2,1)} %bitcast.3), channel_id=1, replica_groups={{0,4,16,20,1,5,17,21,2,6,18,22,3,7,19,23,32,36,48,52,33,37,49,53,34,38,..., dimensions={0} | all-to-all | bytes 4194304 | tf_op jit(solution)/shard_map/all_to_all | solution.py:128
  37.2 0.0 copy-done
  37.2 0.0 copy-done.1
  37.2 8.1 %shard_map.37 = bf16[64,64,256]{2,1,0:T(8,128)(2,1)S(1)} custom-call(bf16[64,64,256]{2,1,0:T(8,128)(2,1)S(1)} %all_to_all.10.tokens, bf16[256,768]{1,0:T(8,128)(2,1)S(1)} %copy-done, bf16[256,256]{1,0:T(8,128)(2,1)S(1)} %copy-done.1), custom_call_target="tpu_custom_call" | custom-call | tf_op jit(solution)/shard_map/pallas_call | solution.py:107
  45.3 33.9 %all_to_all.11 = bf16[64,64,256]{2,1,0:T(8,128)(2,1)S(1)} all-to-all(bf16[64,64,256]{2,1,0:T(8,128)(2,1)S(1)} %shard_map.37), channel_id=1, replica_groups={{0,4,16,20,1,5,17,21,2,6,18,22,3,7,19,23,32,36,48,52,33,37,49,53,34,38,..., dimensions={0} | all-to-all | bytes 4194304 | tf_op jit(solution)/shard_map/all_to_all | solution.py:129
  79.2 1.3 %copy.5 = bf16[16,256,256]{2,1,0:T(8,128)(2,1)} copy(bf16[16,256,256]{2,1,0:T(8,128)(2,1)S(1)} %bitcast.2) | data formatting | bytes 4194304
Async XLA Ops:
  0.0 37.2 %copy-start = (bf16[256,768]{1,0:T(8,128)(2,1)S(1)}, bf16[256,768]{1,0:T(8,128)(2,1)}, u32[]{:S(2)}) copy-start(bf16[256,768]{1,0:T(8,128)(2,1)} %w_qkv.1) | copy-start | bytes 1179652
  0.0 37.2 %copy-start.1 = (bf16[256,256]{1,0:T(8,128)(2,1)S(1)}, bf16[256,256]{1,0:T(8,128)(2,1)}, u32[]{:S(2)}) copy-start(bf16[256,256]{1,0:T(8,128)(2,1)} %w_out.1) | copy-start | bytes 393220

commit v6 on v5

--- a/solution.py
+++ b/solution.py
@@ -23,7 +23,7 @@
     lists = []
     for which in range(share):
         chips = np.roll(index[which], 2 * which, (0, 1, 2))
-        lists.append(chips.transpose(0, 2, 1).reshape(-1).tolist())
+        lists.append(chips.transpose(1, 0, 2).reshape(-1).tolist())
     return lists
 
 

time: 81.1 us -> 80.8 us (level)
    all_to_all x1, blocking collectives: 33.9 us -> 32.7 us  [body(): returned = exchange(attend(arrived, w_qkv, w_out))]
    all_to_all x1, blocking collectives: 37.2 us -> 38.4 us  [body(): exchange(tokens.reshape(members, rows * columns // members, width))]
where the time goes in v6:
time: 80.8 us; the launch traced here: 80.6 us
  blocking collectives  71.1 us (88%)
  Pallas kernels  8.14 us (10%)
  local copies, waits for them, and re-layouts  1.33 us (2%)
    all_to_all x1, blocking collectives, body(): exchange(tokens.reshape(members, rows * columns // members, width))  38.4 us
    all_to_all x1, blocking collectives, body(): returned = exchange(attend(arrived, w_qkv, w_out))  32.7 us
    pallas_call x1, Pallas kernels, attend(): pl.pallas_call(functools.partial(attend_kernel, members, groups, groups,...  8.14 us

profile of v6, /device:TPU:0, one launch (start us, length us, event | category | flops | bytes accessed | tf_op | source)
XLA Modules:
  0.0 80.6 jit_solution(14679263496587345890)
XLA Ops:
  0.0 0.0 copy-start
  0.0 0.0 copy-start.1
  0.0 38.4 %all_to_all.10.tokens = bf16[64,64,256]{2,1,0:T(8,128)(2,1)S(1)} all-to-all(bf16[64,64,256]{2,1,0:T(8,128)(2,1)} %bitcast.3), channel_id=1, replica_groups={{0,1,2,3,32,33,34,35,64,65,66,67,96,97,98,99,4,5,6,7,36,37,38,39,68,69,..., dimensions={0} | all-to-all | bytes 4194304 | tf_op jit(solution)/shard_map/all_to_all | solution.py:128
  38.4 0.0 copy-done
  38.4 0.0 copy-done.1
  38.4 8.1 %shard_map.37 = bf16[64,64,256]{2,1,0:T(8,128)(2,1)S(1)} custom-call(bf16[64,64,256]{2,1,0:T(8,128)(2,1)S(1)} %all_to_all.10.tokens, bf16[256,768]{1,0:T(8,128)(2,1)S(1)} %copy-done, bf16[256,256]{1,0:T(8,128)(2,1)S(1)} %copy-done.1), custom_call_target="tpu_custom_call" | custom-call | tf_op jit(solution)/shard_map/pallas_call | solution.py:107
  46.6 32.7 %all_to_all.11 = bf16[64,64,256]{2,1,0:T(8,128)(2,1)S(1)} all-to-all(bf16[64,64,256]{2,1,0:T(8,128)(2,1)S(1)} %shard_map.37), channel_id=1, replica_groups={{0,1,2,3,32,33,34,35,64,65,66,67,96,97,98,99,4,5,6,7,36,37,38,39,68,69,..., dimensions={0} | all-to-all | bytes 4194304 | tf_op jit(solution)/shard_map/all_to_all | solution.py:129
  79.2 1.3 %copy.5 = bf16[16,256,256]{2,1,0:T(8,128)(2,1)} copy(bf16[16,256,256]{2,1,0:T(8,128)(2,1)S(1)} %bitcast.2) | data formatting | bytes 4194304
Async XLA Ops:
  0.0 38.4 %copy-start = (bf16[256,768]{1,0:T(8,128)(2,1)S(1)}, bf16[256,768]{1,0:T(8,128)(2,1)}, u32[]{:S(2)}) copy-start(bf16[256,768]{1,0:T(8,128)(2,1)} %w_qkv.1) | copy-start | bytes 1179652
  0.0 38.4 %copy-start.1 = (bf16[256,256]{1,0:T(8,128)(2,1)S(1)}, bf16[256,256]{1,0:T(8,128)(2,1)}, u32[]{:S(2)}) copy-start(bf16[256,256]{1,0:T(8,128)(2,1)} %w_out.1) | copy-start | bytes 393220

commit v7 on v6

--- a/solution.py
+++ b/solution.py
@@ -22,7 +22,7 @@
     index = index.transpose(2, 0, 1, 3, 4).reshape(share, 4, 4, lon_count // 2)
     lists = []
     for which in range(share):
-        chips = np.roll(index[which], 2 * which, (0, 1, 2))
+        chips = np.roll(index[which], which, (0, 1, 2))
         lists.append(chips.transpose(1, 0, 2).reshape(-1).tolist())
     return lists
 

time: 80.8 us -> 82.5 us (1.021)
  blocking collectives: 71.1 us -> 72.2 us
    all_to_all x1, blocking collectives: 32.7 us -> 34.1 us  [body(): returned = exchange(attend(arrived, w_qkv, w_out))]
where the time goes in v7:
time: 82.5 us; the launch traced here: 81.6 us
  blocking collectives  72.2 us (88%)
  Pallas kernels  8.13 us (10%)
  local copies, waits for them, and re-layouts  1.33 us (2%)
    all_to_all x1, blocking collectives, body(): exchange(tokens.reshape(members, rows * columns // members, width))  38.1 us
    all_to_all x1, blocking collectives, body(): returned = exchange(attend(arrived, w_qkv, w_out))  34.1 us
    pallas_call x1, Pallas kernels, attend(): pl.pallas_call(functools.partial(attend_kernel, members, groups, groups,...  8.13 us

profile of v7, /device:TPU:0, one launch (start us, length us, event | category | flops | bytes accessed | tf_op | source)
XLA Modules:
  0.0 81.6 jit_solution(10387095320751539441)
XLA Ops:
  0.0 0.0 copy-start
  0.0 0.0 copy-start.1
  0.0 38.1 %all_to_all.10.tokens = bf16[64,64,256]{2,1,0:T(8,128)(2,1)S(1)} all-to-all(bf16[64,64,256]{2,1,0:T(8,128)(2,1)} %bitcast.3), channel_id=1, replica_groups={{0,1,2,3,32,33,34,35,64,65,66,67,96,97,98,99,4,5,6,7,36,37,38,39,68,69,..., dimensions={0} | all-to-all | bytes 4194304 | tf_op jit(solution)/shard_map/all_to_all | solution.py:128
  38.1 0.0 copy-done
  38.1 0.0 copy-done.1
  38.1 8.1 %shard_map.37 = bf16[64,64,256]{2,1,0:T(8,128)(2,1)S(1)} custom-call(bf16[64,64,256]{2,1,0:T(8,128)(2,1)S(1)} %all_to_all.10.tokens, bf16[256,768]{1,0:T(8,128)(2,1)S(1)} %copy-done, bf16[256,256]{1,0:T(8,128)(2,1)S(1)} %copy-done.1), custom_call_target="tpu_custom_call" | custom-call | tf_op jit(solution)/shard_map/pallas_call | solution.py:107
  46.2 34.1 %all_to_all.11 = bf16[64,64,256]{2,1,0:T(8,128)(2,1)S(1)} all-to-all(bf16[64,64,256]{2,1,0:T(8,128)(2,1)S(1)} %shard_map.37), channel_id=1, replica_groups={{0,1,2,3,32,33,34,35,64,65,66,67,96,97,98,99,4,5,6,7,36,37,38,39,68,69,..., dimensions={0} | all-to-all | bytes 4194304 | tf_op jit(solution)/shard_map/all_to_all | solution.py:129
  80.3 1.3 %copy.5 = bf16[16,256,256]{2,1,0:T(8,128)(2,1)} copy(bf16[16,256,256]{2,1,0:T(8,128)(2,1)S(1)} %bitcast.2) | data formatting | bytes 4194304
Async XLA Ops:
  0.0 38.1 %copy-start = (bf16[256,768]{1,0:T(8,128)(2,1)S(1)}, bf16[256,768]{1,0:T(8,128)(2,1)}, u32[]{:S(2)}) copy-start(bf16[256,768]{1,0:T(8,128)(2,1)} %w_qkv.1) | copy-start | bytes 1179652
  0.0 38.1 %copy-start.1 = (bf16[256,256]{1,0:T(8,128)(2,1)S(1)}, bf16[256,256]{1,0:T(8,128)(2,1)}, u32[]{:S(2)}) copy-start(bf16[256,256]{1,0:T(8,128)(2,1)} %w_out.1) | copy-start | bytes 393220
